TPU v7x, 512 devices: a whole 4x4x16 slice. The times are simulated.
512 devices in a mesh: geo: 64 (over z, y), cell: 8 (over x, core).
Axes of the slice: x: 4, y: 4, z: 16, core: 2. Of those that a mesh axis runs over, the one named last changes fastest.
Arguments:
- detail_rows: float32 [8192, 2048], P('geo', 'cell'), may hold values from -60 to 60
- row_block: int32 [8192], P('geo'), may hold values from 0 to 8191, as said below
- block_weight: int32 [8192], P('geo'), may hold values from 1 to 9
- block_group: int32 [8192], P('geo'), may hold values from 0 to 63, as said below
- query_matrix: int32 [2048, 512], P('cell'), may hold values 0 or 1
- query_weight: float32 [512], replicated, may hold values from 0.0048828125 to 0.048828125
- query_noisy: float32 [8192, 512], P('geo'), may hold values from -48 to 48
- group_noisy: float32 [64, 2048], P(None, 'cell'), may hold values from -48 to 48
Outputs:
- solution_field: float32 [8192, 2048], P('geo', 'cell')
- residual: float32 [8192, 2048], P('geo', 'cell')
Inputs may be any that keep to these rules, and one draw needn't show every extreme that they name: row_block is a permutation of all blocks; arrival row r lies on geo index r // 128 and its block lies on geo index (r mod 128) // 2, so each geo index sends 2 rows to each geo index. `block_group`: every group holds exactly 128 blocks.
All inputs are finite; a program needn't handle non-finite values. No bound on the sum of `query_matrix` on one device may be relied on, other than what follows from the above.
Results may differ from a plain program's by a relative error of at most 0.0029.
Values sent between devices are 32-bit elements; how exact they have to be, the bound alone decides.
A program may use at most 64 MiB of HBM per device.

v0:
```python
import jax
import jax.numpy as jnp
from jax import lax
from jax.sharding import PartitionSpec as P

QUERIES = 512
ITERS = 2
BLK_DEV = 128
AGG_WEIGHT = 0.25
HIGHEST_PREC = lax.Precision.HIGHEST
LEADING_DIMS = (((0,), (1,)), ((), ()))


def local(
    detail_rows,
    row_block,
    block_weight,
    block_group,
    query_matrix,
    query_weight,
    query_noisy,
    group_noisy,
):
    geo_index = lax.axis_index("geo")
    sent_ids = row_block.astype(jnp.float32)
    rows_in, ids_in = (
        lax.all_to_all(detail_rows, "geo", split_axis=0, concat_axis=0, tiled=True),
        lax.all_to_all(sent_ids, "geo", split_axis=0, concat_axis=0, tiled=True),
    )
    local_rows = ids_in.astype(jnp.int32) - geo_index * BLK_DEV
    detail = jnp.zeros(detail_rows.shape, jnp.float32).at[local_rows].set(rows_in)
    weight = block_weight.astype(jnp.float32)[:, None]
    queries = query_matrix.astype(jnp.float32)
    group_count = group_noisy.shape[0]
    share_rows = QUERIES // lax.axis_size("cell")

    def squares(vector):
        return lax.psum(jnp.sum(vector * vector), ("geo", "cell"))

    right_side = weight * detail
    right_side = right_side + jnp.dot(
        query_noisy * query_weight[None, :],
        queries.T,
        precision=HIGHEST_PREC,
        preferred_element_type=jnp.float32,
    )
    right_side = right_side + AGG_WEIGHT * group_noisy[block_group]
    solution_field = jnp.zeros_like(right_side)
    residual = right_side
    direction = right_side
    norm_now = squares(residual)
    for iteration in range(ITERS):
        partial_totals = jax.ops.segment_sum(direction, block_group, num_segments=group_count)
        totals = lax.psum(partial_totals, "geo")
        estimate = direction
        share_part = lax.psum_scatter(
            lax.dot_general(
                queries,
                estimate,
                LEADING_DIMS,
                precision=HIGHEST_PREC,
                preferred_element_type=jnp.float32,
            ),
            "cell",
            scatter_dimension=0,
            tiled=True,
        )
        scales = lax.dynamic_slice_in_dim(
            query_weight, lax.axis_index("cell") * share_rows, share_rows, 0
        )
        share_part = share_part * scales[:, None]
        spread_back = lax.dot_general(
            lax.all_gather(share_part, "cell", axis=0, tiled=True),
            queries,
            LEADING_DIMS,
            precision=HIGHEST_PREC,
            preferred_element_type=jnp.float32,
        )
        image_vec = weight * direction + spread_back + AGG_WEIGHT * totals[block_group]
        step_size = norm_now / lax.psum(jnp.sum(direction * image_vec), ("geo", "cell"))
        solution_field = solution_field + step_size * direction
        residual = residual - step_size * image_vec
        norm_next = squares(residual)
        direction = residual + norm_next / norm_now * direction
        norm_now = norm_next
    return (solution_field, residual)


def solution(mesh):
    return jax.shard_map(
        local,
        mesh=mesh,
        in_specs=(
            P("geo", "cell"),
            P("geo"),
            P("geo"),
            P("geo"),
            P("cell", None),
            P(),
            P("geo", None),
            P(None, "cell"),
        ),
        out_specs=(P("geo", "cell"), P("geo", "cell")),
        check_vma=False,
    )
```

profile of v0, /device:TPU:1, one launch (start us, length us, event | category | flops | bytes accessed | tf_op | source)
XLA Modules:
  0.0 915.7 jit_solution(15356650263555236824)
XLA Ops:
  8.0 0.0 copy-start
  8.0 0.7 convert_element_type.21
  8.7 0.8 all_to_all.14
  9.5 19.3 %all-to-all-start = ((f32[64,2,1]{1,2,0:T(1,128)}), f32[64,2,1]{1,2,0:T(1,128)S(1)}, u32[]{:S(2)}, u32[]{:S(2)}) async-start(f32[64,2,1]{1,2,0:T(1,128)} %bitcast), calls=%async_computation | async-start | bytes 65536 | tf_op jit(solution)/shard_map/all_to_all | solution.py:28
  28.7 1.6 all_to_all.16
  30.4 11.7 %all-to-all-done = f32[64,2,1]{1,2,0:T(1,128)S(1)} async-done(((f32[64,2,1]{1,2,0:T(1,128)}), f32[64,2,1]{1,2,0:T(1,128)S(1)}, u32[]{:S(2)}, u32[]{:S(2)}) %all-to-all-start) | async-done | bytes 544 | tf_op jit(solution)/shard_map/all_to_all | solution.py:28
  42.1 4.6 all-to-all-start.1
  46.8 0.0 all-reduce.4.cloned.1.call-start
  46.8 0.6 copy-done.4
  47.5 0.8 gather_fusion
  48.3 0.1 subtract_reduce_fusion
  48.4 0.1 sub.24
  48.6 13.3 %all-to-all-done.1 = f32[64,2,256]{2,1,0:T(2,128)S(1)} async-done(((f32[64,2,256]{2,1,0:T(2,128)}), f32[64,2,256]{2,1,0:T(2,128)S(1)}, u32[]{:S(2)}, u32[]{:S(2)}) %all-to-all-start.1) | async-done | bytes 131104 | tf_op jit(solution)/shard_map/all_to_all | solution.py:27
  61.9 0.1 reshape.64
  62.0 0.0 copy-start.3
  62.0 1.0 scatter_custom_fusion
  63.1 0.7 fusion.2
  63.8 1.8 scatter_custom_fusion.1
  65.6 0.0 all-reduce.4.cloned.1.call-update
  65.6 0.0 reduce-scatter.7.cloned.1.call-start
  65.7 0.4 convolution_bitcast_fusion.1
  66.1 0.8 copy.16
  67.0 0.0 reduce-scatter.7.cloned.1.call-update
  67.0 0.0 all-reduce.6.cloned.1.call-start
  67.0 0.1 dynamic_slice.4
  67.1 238.7 %all-reduce.4.cloned.1.call-done = f32[64,256]{1,0:T(8,128)} async-done(((f32[64,256]{1,0:T(8,128)}), f32[64,256]{1,0:T(8,128)}) %all-reduce.4.cloned.1.call-update) | async-done | bytes 65552 | tf_op jit(solution)/shard_map/psum | solution.py:54
  305.8 1.6 gather_fusion.1
  307.4 0.0 reduce-scatter.7.cloned.1.call-done
  307.4 0.8 broadcast_multiply_fusion.1
  308.3 23.9 %all_gather.6 = f32[512,128]{1,0:T(8,128)S(1)} all-gather(f32[64,128]{1,0:T(8,128)S(1)} %broadcast_multiply_fusion.1), channel_id=1, replica_groups=mesh['geo'=64,'cell'=8] {'cell'}, dimensions={0}, use_global_device_ids=true | all-gather | bytes 294912 | tf_op jit(solution)/shard_map/all_gather | solution.py:73
  332.2 1.2 multiply_reduce_fusion.2
  333.4 100.5 %all-reduce = (f32[]{:T(128)}, f32[]{:T(128)}) all-reduce(f32[]{:T(128)} %get-tuple-element.3, f32[]{:T(128)} %get-tuple-element.2), channel_id=1, replica_groups=mesh['geo'=64,'cell'=8] {'geo','cell'}, use_global_device_ids=true, to_apply=%region_2.0 | all-reduce | flops 2 | bytes 16 | tf_op jit(solution)/shard_map/psum | solution.py:38
  435.2 0.6 multiply_reduce_fusion.1
  435.8 99.4 %psum.45 = f32[]{:T(128)} all-reduce(f32[]{:T(128)} %multiply_reduce_fusion.1), channel_id=1, replica_groups=mesh['geo'=64,'cell'=8] {'geo','cell'}, use_global_device_ids=true, to_apply=%region_9.0 | all-reduce | flops 1 | bytes 8 | tf_op jit(solution)/shard_map/psum | solution.py:38
  536.6 1.8 scatter_custom_fusion.2
  538.4 0.0 all-reduce.6.cloned.1.call-update
  538.4 0.0 reduce-scatter.9.cloned.1.call-start
  538.5 0.4 convolution_bitcast_fusion
  538.9 0.8 copy.18
  539.7 0.0 reduce-scatter.9.cloned.1.call-update
  539.8 238.5 %all-reduce.6.cloned.1.call-done = f32[64,256]{1,0:T(8,128)} async-done(((f32[64,256]{1,0:T(8,128)}), f32[64,256]{1,0:T(8,128)}) %all-reduce.6.cloned.1.call-update) | async-done | bytes 65552 | tf_op jit(solution)/shard_map/psum | solution.py:54
  778.3 1.6 gather_fusion.2
  779.9 0.0 reduce-scatter.9.cloned.1.call-done
  779.9 0.8 broadcast_multiply_fusion
  780.7 23.9 %all_gather.7 = f32[512,128]{1,0:T(8,128)S(1)} all-gather(f32[64,128]{1,0:T(8,128)S(1)} %broadcast_multiply_fusion), channel_id=1, replica_groups=mesh['geo'=64,'cell'=8] {'cell'}, dimensions={0}, use_global_device_ids=true | all-gather | bytes 294912 | tf_op jit(solution)/shard_map/all_gather | solution.py:73
  804.6 1.2 multiply_reduce_fusion
  805.8 100.4 %psum.47 = f32[]{:T(128)} all-reduce(f32[]{:T(128)} %get-tuple-element.9), channel_id=1, replica_groups=mesh['geo'=64,'cell'=8] {'geo','cell'}, use_global_device_ids=true, to_apply=%region_14.0 | all-reduce | flops 1 | bytes 8 | tf_op jit(solution)/shard_map/psum | solution.py:80
  907.5 0.7 multiply_subtract_fusion
  (14 shorter events, 0.1 us)
Async XLA Ops:
  8.0 39.5 %copy-start = (f32[64,256]{1,0:T(8,128)S(1)}, f32[64,256]{1,0:T(8,128)}, u32[]{:S(2)}) copy-start(f32[64,256]{1,0:T(8,128)} %param.15) | copy-start | bytes 196612
  9.5 32.7 %all-to-all-start = ((f32[64,2,1]{1,2,0:T(1,128)}), f32[64,2,1]{1,2,0:T(1,128)S(1)}, u32[]{:S(2)}, u32[]{:S(2)}) async-start(f32[64,2,1]{1,2,0:T(1,128)} %bitcast), calls=%async_computation | async-start | bytes 65536 | tf_op jit(solution)/shard_map/all_to_all | solution.py:28
  30.4 16.4 %copy-start.5 = (s32[128]{0:T(128)S(1)}, s32[128]{0:T(128)}, u32[]{:S(2)}) copy-start(s32[128]{0:T(128)} %param.11) | copy-start | bytes 1540
  42.1 19.8 %all-to-all-start.1 = ((f32[64,2,256]{2,1,0:T(2,128)}), f32[64,2,256]{2,1,0:T(2,128)S(1)}, u32[]{:S(2)}, u32[]{:S(2)}) async-start(f32[64,2,256]{2,1,0:T(2,128)} %all_to_all.16), calls=%async_computation.1 | async-start | bytes 262144 | tf_op jit(solution)/shard_map/all_to_all | solution.py:27
  46.8 259.0 %all-reduce.4.cloned.1.call-start = ((), (), s32[]{:S(2)}) async-start(), calls=%async_computation.4 | async-start | bytes 131072 | tf_op jit(solution)/shard_map/psum | solution.py:54
  46.8 0.7 copy-start.4
  47.5 15.6 %copy-start.1 = (s32[256,512]{1,0:T(8,128)S(1)}, s32[256,512]{1,0:T(8,128)}, u32[]{:S(2)}) copy-start(s32[256,512]{1,0:T(8,128)} %param.12) | copy-start | bytes 1572868
  48.3 14.8 %copy-start.2 = (f32[128,512]{1,0:T(8,128)S(1)}, f32[128,512]{1,0:T(8,128)}, u32[]{:S(2)}) copy-start(f32[128,512]{1,0:T(8,128)} %param.14) | copy-start | bytes 786436
  62.0 1.1 copy-start.3
  65.6 241.8 %reduce-scatter.7.cloned.1.call-start = ((), (), s32[]{:S(2)}) async-start(), calls=%async_computation.6 | async-start | bytes 294912 | tf_op jit(solution)/shard_map/reduce_scatter | solution.py:56
  67.0 711.3 %all-reduce.6.cloned.1.call-start = ((), (), s32[]{:S(2)}) async-start(), calls=%async_computation.5 | async-start | bytes 131072 | tf_op jit(solution)/shard_map/psum | solution.py:54
  538.4 241.5 %reduce-scatter.9.cloned.1.call-start = ((), (), s32[]{:S(2)}) async-start(), calls=%async_computation.7 | async-start | bytes 294912 | tf_op jit(solution)/shard_map/reduce_scatter | solution.py:56
Sparse Core Ops, SparseCore 0:
  65.8 239.9 all-reduce.3
  538.5 239.6 all-reduce.5
Sparse Core Ops, SparseCore 1:
  68.9 29.8 reduce-scatter.6
  541.9 28.9 reduce-scatter.8
where the time goes:
time: 917 us; the launch traced here: 916 us
  waiting for transfers between devices  502 us (55%)
  blocking collectives  348 us (38%)
  starting transfers between devices  24.1 us (3%)
  between operations  19.7 us (2%)
  local copies, waits for them, and re-layouts  10 us (1%)
    psum x2, waiting for transfers between devices, local(): totals = lax.psum(partial_totals, 'geo')  477 us
    psum x2, blocking collectives, squares(): return lax.psum(jnp.sum(vector * vector), ('geo', 'cell'))  200 us
    psum x1, blocking collectives, local(): lax.psum(jnp.sum(direction * image_vec), ('geo', 'cell'))  100 us
    all_gather x2, blocking collectives, local(): lax.all_gather(share_part, 'cell', axis=0, tiled=True)  47.8 us
    all_to_all x1, starting transfers between devices, local(): lax.all_to_all(sent_ids, 'geo', split_axis=0, concat_axis=0, tiled=True)  19.3 us
  transfers between devices with their start and end apart: 6, of which 4 were waited for; matrix products, arithmetic and copies ran while one was open for 1% of the time, Pallas kernels for 0%

commit v1 on v0

--- a/solution.py
+++ b/solution.py
@@ -9,6 +9,32 @@
 AGG_WEIGHT = 0.25
 HIGHEST_PREC = lax.Precision.HIGHEST
 LEADING_DIMS = (((0,), (1,)), ((), ()))
+
+
+def wait_the_sample(z, on_dim):
+    moved = list(z.shape[1:])
+    moved[on_dim] *= z.shape[0]
+    return jnp.moveaxis(z, 0, on_dim).reshape(moved)
+
+
+def read_rails(my_tile, dev_axis, dim_k):
+    num_devices = lax.axis_size(dev_axis)
+    blocks_here = [(d, (d + 1) % num_devices) for d in range(num_devices)]
+    row_list = [(w, tick) for tick, w in blocks_here]
+    y_new, a_next = ([], [])
+    for s in range(num_devices - 1):
+        if s % 2 == 0:
+            y_new.append(
+                lax.ppermute(y_new[-1] if y_new else my_tile, axis_name=dev_axis, perm=blocks_here)
+            )
+        else:
+            a_next.append(
+                lax.ppermute(a_next[-1] if a_next else my_tile, axis_name=dev_axis, perm=row_list)
+            )
+    local_part = jnp.stack([*y_new[::-1], my_tile, *a_next], axis=0)
+    near = lax.axis_index(dev_axis) - len(y_new)
+    local_part = local_part[(jnp.arange(num_devices) - near) % num_devices]
+    return wait_the_sample(local_part, dim_k)
 
 
 def local(
@@ -70,7 +96,7 @@
         )
         share_part = share_part * scales[:, None]
         spread_back = lax.dot_general(
-            lax.all_gather(share_part, "cell", axis=0, tiled=True),
+            read_rails(share_part, "cell", dim_k=0),
             queries,
             LEADING_DIMS,
             precision=HIGHEST_PREC,

time: 917 us -> 991 us (1.081)
  waiting for transfers between devices: 502 us -> 584 us
  blocking collectives: 348 us -> 299 us
  starting transfers between devices: 24.1 us -> 63.8 us
    reduce_scatter x2, waiting for transfers between devices: 0.05 us -> 58.2 us  [local(): lax.psum_scatter(lax.dot_general(queries, estimate, LEADING_DIMS, precisi...]
    all_gather x2 -> x0, blocking collectives: 47.8 us -> none  [local(): lax.all_gather(share_part, 'cell', axis=0, tiled=True)]
    ppermute x0 -> x14, starting transfers between devices: none -> 39.7 us  [the longest x6 37.6 us: read_rails(): lax.ppermute(a_next[-1] if a_next else my_tile, axis_name=dev_axis, perm=...]
    psum x2, waiting for transfers between devices: 477 us -> 490 us  [local(): totals = lax.psum(partial_totals, 'geo')]
    ppermute x0 -> x14, waiting for transfers between devices: none -> 10.4 us  [the longest x8 5.93 us: read_rails(): lax.ppermute(y_new[-1] if y_new else my_tile, axis_name=dev_axis, perm=bl...]
  transfers between devices with their start and end apart: 6 -> 20, of which waited for: 4 -> 12; matrix products, arithmetic and copies ran while one was open for 1% -> 1% of each run, Pallas kernels for 0% -> 0%
where the time goes in v1:
time: 991 us; the launch traced here: 990 us
  waiting for transfers between devices  584 us (59%)
  blocking collectives  299 us (30%)
  starting transfers between devices  63.8 us (6%)
  between operations  19.6 us (2%)
  local copies, waits for them, and re-layouts  12.7 us (1%)
    psum x2, waiting for transfers between devices, local(): totals = lax.psum(partial_totals, 'geo')  490 us
    psum x2, blocking collectives, squares(): return lax.psum(jnp.sum(vector * vector), ('geo', 'cell'))  199 us
    psum x1, blocking collectives, local(): lax.psum(jnp.sum(direction * image_vec), ('geo', 'cell'))  99.7 us
    reduce_scatter x2, waiting for transfers between devices, local(): lax.psum_scatter(lax.dot_general(queries, estimate, LEADING_DIMS, precisi...  58.2 us
    ppermute x6, starting transfers between devices, read_rails(): lax.ppermute(a_next[-1] if a_next else my_tile, axis_name=dev_axis, perm=...  37.6 us
  transfers between devices with their start and end apart: 20, of which 12 were waited for; matrix products, arithmetic and copies ran while one was open for 1% of the time, Pallas kernels for 0%

profile of v1, /device:TPU:1, one launch (start us, length us, event | category | flops | bytes accessed | tf_op | source)
XLA Modules:
  0.0 990.5 jit_solution(12859310589501012251)
XLA Ops:
  8.0 0.7 convert_element_type.21
  8.7 0.8 all_to_all.14
  9.5 19.3 %all-to-all-start = ((f32[64,2,1]{1,2,0:T(1,128)}), f32[64,2,1]{1,2,0:T(1,128)S(1)}, u32[]{:S(2)}, u32[]{:S(2)}) async-start(f32[64,2,1]{1,2,0:T(1,128)} %bitcast), calls=%async_computation | async-start | bytes 65536 | tf_op jit(solution)/shard_map/all_to_all | solution.py:54
  28.7 1.6 all_to_all.16
  30.4 11.7 %all-to-all-done = f32[64,2,1]{1,2,0:T(1,128)S(1)} async-done(((f32[64,2,1]{1,2,0:T(1,128)}), f32[64,2,1]{1,2,0:T(1,128)S(1)}, u32[]{:S(2)}, u32[]{:S(2)}) %all-to-all-start) | async-done | bytes 544 | tf_op jit(solution)/shard_map/all_to_all | solution.py:54
  42.1 4.6 all-to-all-start.1
  46.8 0.6 copy-done.6
  47.5 0.8 gather_fusion
  48.6 13.3 %all-to-all-done.1 = f32[64,2,256]{2,1,0:T(2,128)S(1)} async-done(((f32[64,2,256]{2,1,0:T(2,128)}), f32[64,2,256]{2,1,0:T(2,128)S(1)}, u32[]{:S(2)}, u32[]{:S(2)}) %all-to-all-start.1) | async-done | bytes 131104 | tf_op jit(solution)/shard_map/all_to_all | solution.py:53
  62.0 1.0 scatter_custom_fusion
  63.1 0.7 fusion.2
  64.2 0.8 copy.16
  65.2 29.3 %reduce-scatter.7.cloned.1.call-done = f32[64,128]{1,0:T(8,128)} async-done(((f32[512,128]{1,0:T(8,128)}), f32[64,128]{1,0:T(8,128)}) %reduce-scatter.7.cloned.1.call-update) | async-done | bytes 32784 | tf_op jit(solution)/shard_map/reduce_scatter | solution.py:82
  94.5 0.8 broadcast_multiply_fusion.1
  95.6 2.6 collective-permute-done
  98.2 0.7 collective-permute-start.1
  99.0 3.1 collective-permute-start.4
  102.1 0.7 collective-permute-done.1
  102.8 1.8 scatter_custom_fusion.1
  104.7 3.9 collective-permute-start.5
  108.6 247.2 %all-reduce.4.cloned.1.call-done = f32[64,256]{1,0:T(8,128)} async-done(((f32[64,256]{1,0:T(8,128)}), f32[64,256]{1,0:T(8,128)}) %all-reduce.4.cloned.1.call-update) | async-done | bytes 65552 | tf_op jit(solution)/shard_map/psum | solution.py:80
  355.8 1.6 gather_fusion.2
  357.4 11.9 %collective-permute-start.6 = (f32[64,128]{1,0:T(8,128)S(1)}, f32[64,128]{1,0:T(8,128)S(1)}, u32[]{:S(2)}, u32[]{:S(2)}) collective-permute-start(f32[64,128]{1,0:T(8,128)S(1)} %collective-permute-done.5), channel_id=1, source_target_pairs={{1,0},{2,1},{3,2},{4,3},{5,4},{6,5},{7,6},{0,7},{9,8},{10,9},{11,1... | collective-permute-start | bytes 98312 | tf_op jit(solution)/shard_map/ppermute | solution.py:32
  369.4 0.7 copy-done.3
  370.2 1.8 collective-permute-done.6
  372.0 0.6 gather_fusion.1
  372.6 1.2 multiply_reduce_fusion.2
  373.8 99.8 %all-reduce = (f32[]{:T(128)}, f32[]{:T(128)}) all-reduce(f32[]{:T(128)} %get-tuple-element.3, f32[]{:T(128)} %get-tuple-element.2), channel_id=1, replica_groups=mesh['geo'=64,'cell'=8] {'geo','cell'}, use_global_device_ids=true, to_apply=%region_2.0 | all-reduce | flops 2 | bytes 16 | tf_op jit(solution)/shard_map/psum | solution.py:64
  474.9 0.6 multiply_reduce_fusion.1
  475.6 99.4 %psum.45 = f32[]{:T(128)} all-reduce(f32[]{:T(128)} %multiply_reduce_fusion.1), channel_id=1, replica_groups=mesh['geo'=64,'cell'=8] {'geo','cell'}, use_global_device_ids=true, to_apply=%region_9.10 | all-reduce | flops 1 | bytes 8 | tf_op jit(solution)/shard_map/psum | solution.py:64
  576.7 0.8 copy.18
  577.6 29.0 %reduce-scatter.9.cloned.1.call-done = f32[64,128]{1,0:T(8,128)} async-done(((f32[512,128]{1,0:T(8,128)}), f32[64,128]{1,0:T(8,128)}) %reduce-scatter.9.cloned.1.call-update) | async-done | bytes 32784 | tf_op jit(solution)/shard_map/reduce_scatter | solution.py:82
  606.5 0.8 broadcast_multiply_fusion
  607.7 2.6 collective-permute-done.7
  610.3 0.7 collective-permute-start.8
  611.0 1.8 scatter_custom_fusion.2
  612.9 3.1 collective-permute-start.11
  616.0 0.9 collective-permute-done.11
  616.9 3.7 collective-permute-start.12
  620.6 242.8 %all-reduce.6.cloned.1.call-done = f32[64,256]{1,0:T(8,128)} async-done(((f32[64,256]{1,0:T(8,128)}), f32[64,256]{1,0:T(8,128)}) %all-reduce.6.cloned.1.call-update) | async-done | bytes 65552 | tf_op jit(solution)/shard_map/psum | solution.py:80
  863.4 1.6 gather_fusion.4
  865.0 11.9 %collective-permute-start.13 = (f32[64,128]{1,0:T(8,128)S(1)}, f32[64,128]{1,0:T(8,128)S(1)}, u32[]{:S(2)}, u32[]{:S(2)}) collective-permute-start(f32[64,128]{1,0:T(8,128)S(1)} %collective-permute-done.12), channel_id=1, source_target_pairs={{1,0},{2,1},{3,2},{4,3},{5,4},{6,5},{7,6},{0,7},{9,8},{10,9},{11,1... | collective-permute-start | bytes 98312 | tf_op jit(solution)/shard_map/ppermute | solution.py:32
  876.9 0.7 copy-done.4
  877.8 1.8 collective-permute-done.13
  879.6 0.6 gather_fusion.3
  880.1 1.2 multiply_reduce_fusion
  881.3 99.7 %psum.47 = f32[]{:T(128)} all-reduce(f32[]{:T(128)} %get-tuple-element.9), channel_id=1, replica_groups=mesh['geo'=64,'cell'=8] {'geo','cell'}, use_global_device_ids=true, to_apply=%region_14.15 | all-reduce | flops 1 | bytes 8 | tf_op jit(solution)/shard_map/psum | solution.py:106
  982.3 0.7 multiply_subtract_fusion
  (64 shorter events, 2.5 us)
Async XLA Ops:
  8.0 39.5 %copy-start = (f32[64,256]{1,0:T(8,128)S(1)}, f32[64,256]{1,0:T(8,128)}, u32[]{:S(2)}) copy-start(f32[64,256]{1,0:T(8,128)} %param.15) | copy-start | bytes 196612
  9.5 32.7 %all-to-all-start = ((f32[64,2,1]{1,2,0:T(1,128)}), f32[64,2,1]{1,2,0:T(1,128)S(1)}, u32[]{:S(2)}, u32[]{:S(2)}) async-start(f32[64,2,1]{1,2,0:T(1,128)} %bitcast), calls=%async_computation | async-start | bytes 65536 | tf_op jit(solution)/shard_map/all_to_all | solution.py:54
  30.4 16.4 %copy-start.7 = (s32[128]{0:T(128)S(1)}, s32[128]{0:T(128)}, u32[]{:S(2)}) copy-start(s32[128]{0:T(128)} %param.11) | copy-start | bytes 1540
  42.1 19.8 %all-to-all-start.1 = ((f32[64,2,256]{2,1,0:T(2,128)}), f32[64,2,256]{2,1,0:T(2,128)S(1)}, u32[]{:S(2)}, u32[]{:S(2)}) async-start(f32[64,2,256]{2,1,0:T(2,128)} %all_to_all.16), calls=%async_computation.1 | async-start | bytes 262144 | tf_op jit(solution)/shard_map/all_to_all | solution.py:53
  46.8 47.7 %reduce-scatter.7.cloned.1.call-start = ((), (), s32[]{:S(2)}) async-start(), calls=%async_computation.6 | async-start | bytes 294912 | tf_op jit(solution)/shard_map/reduce_scatter | solution.py:82
  46.8 0.7 copy-start.6
  47.5 15.6 %copy-start.1 = (s32[256,512]{1,0:T(8,128)S(1)}, s32[256,512]{1,0:T(8,128)}, u32[]{:S(2)}) copy-start(s32[256,512]{1,0:T(8,128)} %param.12) | copy-start | bytes 1572868
  48.3 14.8 %copy-start.2 = (f32[128,512]{1,0:T(8,128)S(1)}, f32[128,512]{1,0:T(8,128)}, u32[]{:S(2)}) copy-start(f32[128,512]{1,0:T(8,128)} %param.14) | copy-start | bytes 786436
  62.0 1.1 copy-start.5
  65.1 290.7 %all-reduce.4.cloned.1.call-start = ((), (), s32[]{:S(2)}) async-start(), calls=%async_computation.4 | async-start | bytes 131072 | tf_op jit(solution)/shard_map/psum | solution.py:80
  95.3 2.9 collective-permute-start
  98.2 4.6 collective-permute-start.1
  99.0 5.7 collective-permute-start.4
  102.8 5.8 collective-permute-start.2
  104.7 501.9 %reduce-scatter.9.cloned.1.call-start = ((), (), s32[]{:S(2)}) async-start(), calls=%async_computation.7 | async-start | bytes 294912 | tf_op jit(solution)/shard_map/reduce_scatter | solution.py:82
  104.7 252.7 %collective-permute-start.5 = (f32[64,128]{1,0:T(8,128)S(1)}, f32[64,128]{1,0:T(8,128)S(1)}, u32[]{:S(2)}, u32[]{:S(2)}) collective-permute-start(f32[64,128]{1,0:T(8,128)S(1)} %collective-permute-done.4), channel_id=1, source_target_pairs={{1,0},{2,1},{3,2},{4,3},{5,4},{6,5},{7,6},{0,7},{9,8},{10,9},{11,1... | collective-permute-start | bytes 98312 | tf_op jit(solution)/shard_map/ppermute | solution.py:32
  108.6 260.7 %collective-permute-start.3 = (f32[64,128]{1,0:T(8,128)S(1)}, f32[64,128]{1,0:T(8,128)S(1)}, u32[]{:S(2)}, u32[]{:S(2)}) collective-permute-start(f32[64,128]{1,0:T(8,128)S(1)} %collective-permute-done.2), channel_id=1, source_target_pairs={{0,1},{1,2},{2,3},{3,4},{4,5},{5,6},{6,7},{7,0},{8,9},{9,10},{10,1... | collective-permute-start | bytes 98312 | tf_op jit(solution)/shard_map/ppermute | solution.py:28
  357.4 14.6 %collective-permute-start.6 = (f32[64,128]{1,0:T(8,128)S(1)}, f32[64,128]{1,0:T(8,128)S(1)}, u32[]{:S(2)}, u32[]{:S(2)}) collective-permute-start(f32[64,128]{1,0:T(8,128)S(1)} %collective-permute-done.5), channel_id=1, source_target_pairs={{1,0},{2,1},{3,2},{4,3},{5,4},{6,5},{7,6},{0,7},{9,8},{10,9},{11,1... | collective-permute-start | bytes 98312 | tf_op jit(solution)/shard_map/ppermute | solution.py:32
  369.3 0.8 copy-start.3
  577.5 285.8 %all-reduce.6.cloned.1.call-start = ((), (), s32[]{:S(2)}) async-start(), calls=%async_computation.5 | async-start | bytes 131072 | tf_op jit(solution)/shard_map/psum | solution.py:80
  607.4 2.9 collective-permute-start.7
  610.3 5.7 collective-permute-start.8
  612.9 4.0 collective-permute-start.11
  616.0 4.6 collective-permute-start.9
  616.9 248.1 %collective-permute-start.12 = (f32[64,128]{1,0:T(8,128)S(1)}, f32[64,128]{1,0:T(8,128)S(1)}, u32[]{:S(2)}, u32[]{:S(2)}) collective-permute-start(f32[64,128]{1,0:T(8,128)S(1)} %collective-permute-done.11), channel_id=1, source_target_pairs={{1,0},{2,1},{3,2},{4,3},{5,4},{6,5},{7,6},{0,7},{9,8},{10,9},{11,1... | collective-permute-start | bytes 98312 | tf_op jit(solution)/shard_map/ppermute | solution.py:32
  620.6 256.3 %collective-permute-start.10 = (f32[64,128]{1,0:T(8,128)S(1)}, f32[64,128]{1,0:T(8,128)S(1)}, u32[]{:S(2)}, u32[]{:S(2)}) collective-permute-start(f32[64,128]{1,0:T(8,128)S(1)} %collective-permute-done.9), channel_id=1, source_target_pairs={{0,1},{1,2},{2,3},{3,4},{4,5},{5,6},{6,7},{7,0},{8,9},{9,10},{10,1... | collective-permute-start | bytes 98312 | tf_op jit(solution)/shard_map/ppermute | solution.py:28
  865.0 14.6 %collective-permute-start.13 = (f32[64,128]{1,0:T(8,128)S(1)}, f32[64,128]{1,0:T(8,128)S(1)}, u32[]{:S(2)}, u32[]{:S(2)}) collective-permute-start(f32[64,128]{1,0:T(8,128)S(1)} %collective-permute-done.12), channel_id=1, source_target_pairs={{1,0},{2,1},{3,2},{4,3},{5,4},{6,5},{7,6},{0,7},{9,8},{10,9},{11,1... | collective-permute-start | bytes 98312 | tf_op jit(solution)/shard_map/ppermute | solution.py:32
  876.9 0.8 copy-start.4
Sparse Core Ops, SparseCore 0:
  65.2 29.2 reduce-scatter.6
  577.7 28.8 reduce-scatter.8
Sparse Core Ops, SparseCore 1:
  104.8 251.0 all-reduce.3
  613.0 250.3 all-reduce.5
